TPU v7x, 32 devices: a whole 2x2x4 slice. The times are simulated.
32 devices in a mesh: grp: 8 (over z, x), sp: 4 (over y, core).
Axes of the slice: x: 2, y: 2, z: 4, core: 2. Of those that a mesh axis runs over, the one named last changes fastest.
Arguments:
- queries: bfloat16 [5120, 4096], P(('grp', 'sp')), may hold values from -128 to 128
- fresh_key_values: bfloat16 [5120, 1024], P(('grp', 'sp')), may hold values from -4 to 4
- cache: bfloat16 [8, 4, 512, 256], P('grp', 'sp'), may hold values from -4 to 4
- lengths: int32 [8, 4], P('grp', 'sp'), may hold values from 1 to 160, 512 in all within a row
- out_weight: bfloat16 [4096, 2048], P('sp'), may hold values from -1 to 1
- residual: bfloat16 [5120, 2048], P(('grp', 'sp')), may hold values from -36 to 36
- norm_gain: float32 [2048], replicated, may hold values from 0.1 to 1.9
- expert_ids: int32 [5120, 8], P(('grp', 'sp')), may hold values from 0 to 31, all different within a row; in each aligned block of 160 rows (0 to 159, 160 to 319, ...) at most 64 rows name the same one
- gate_values: float32 [5120, 8], P(('grp', 'sp')), may hold values from 0.05 to 0.5
- up_gate_weight: bfloat16 [32, 2048, 1536], P(('grp', 'sp')), may hold values from -0.125 to 0.125
- down_weight: bfloat16 [32, 768, 2048], P(('grp', 'sp')), may hold values from -0.21875 to 0.21875
Outputs:
- attended: bfloat16 [5120, 2048], P(('grp', 'sp'))
- moe_out: bfloat16 [5120, 2048], P(('grp', 'sp'))
Inputs may be any that keep to these rules, and one draw needn't show every extreme that they name: Each group's 4 lengths sum to 512, and in every group one device has exactly 160. `expert_ids`: each slot names 8 different experts; among the 160 slots of one device no expert is named more than 64 times, and one expert is named exactly 64 times by the slots of some device.
All inputs are finite; a program needn't handle non-finite values.
Results may differ from a plain program's by a relative error of at most 0.02.
Values may be sent and summed in bfloat16 or wider, within the bound.
No kernel may reach another device: no remote copies, remote signals or barrier semaphores. Data moves between devices by JAX's collectives and lax.ppermute only.
A program may use at most 128 MiB of HBM per device.

v0:
```python
import math

import jax
import jax.numpy as jnp
from jax import lax
from jax.sharding import PartitionSpec as P


def partner_2(value, axis, bit):
    mask = 2**bit
    pairs = [(source, source ^ mask) for source in range(lax.axis_size(axis))]
    return lax.ppermute(value, axis, pairs)


def per_device(
    queries,
    fresh_key_values,
    cache,
    lengths,
    out_weight,
    residual,
    norm_gain,
    expert_ids,
    gate_values,
    up_gate_weight,
    down_weight,
):
    seq_devices = lax.axis_size("sp")
    slot_rows = queries.shape[0]
    head_width = cache.shape[-1] // 2
    model_width = residual.shape[1]
    kv_heads = fresh_key_values.shape[1] // (2 * head_width)
    repeat = seq_devices // kv_heads
    keys_new = fresh_key_values[:, : kv_heads * head_width].reshape(
        slot_rows, kv_heads, 1, head_width
    )
    values_new = fresh_key_values[:, kv_heads * head_width :].reshape(
        slot_rows, kv_heads, 1, head_width
    )
    paired = jnp.concatenate([keys_new, values_new], axis=3)
    spread = jnp.broadcast_to(paired, (slot_rows, kv_heads, repeat, 2 * head_width)).reshape(
        slot_rows, seq_devices * 2 * head_width
    )
    all_lengths = lax.all_gather(lengths, "sp", axis=1, tiled=True)
    queries_by_head, head_kv = (
        lax.all_to_all(queries, "sp", split_axis=1, concat_axis=0, tiled=True),
        lax.all_to_all(spread, "sp", split_axis=1, concat_axis=0, tiled=True),
    )
    cache_block = cache[0, 0]
    my_index = lax.axis_index("sp")
    for bit_pos in range(repeat.bit_length() - 1):
        partner = partner_2(cache_block, "sp", bit_pos)
        is_upper = my_index // 2**bit_pos % 2 == 1
        cache_block = jnp.where(
            is_upper,
            jnp.concatenate([partner, cache_block], axis=0),
            jnp.concatenate([cache_block, partner], axis=0),
        )
    stretch_lens = all_lengths[0]
    offsets = jnp.cumsum(stretch_lens) - stretch_lens
    rows_of_group = queries_by_head.shape[0]
    slot_ids = jnp.arange(rows_of_group, dtype=jnp.int32)
    source = slot_ids // slot_rows
    within = slot_ids % slot_rows
    from_device = source[:, None] == jnp.arange(seq_devices, dtype=jnp.int32)[None, :]
    is_live = within < jnp.sum(jnp.where(from_device, stretch_lens[None, :], 0), axis=1)
    position = within + jnp.sum(jnp.where(from_device, offsets[None, :], 0), axis=1)
    per_dev = queries_by_head.shape[1] // head_width
    cache_len = cache_block.shape[0]
    key_all = jnp.concatenate([cache_block[:, :head_width], head_kv[:, :head_width]], axis=0)
    value_all = jnp.concatenate([cache_block[:, head_width:], head_kv[:, head_width:]], axis=0)
    block_count = 2 if rows_of_group % 2 == 0 and rows_of_group >= 1024 else 1
    block_rows = rows_of_group // block_count

    def attend(parts):
        query_block, place_block = parts
        scores = jnp.einsum(
            "rhd,kd->hrk", query_block, key_all, preferred_element_type=jnp.float32
        ) / math.sqrt(head_width)
        allowed = jnp.concatenate(
            [
                jnp.ones((block_rows, cache_len), dtype=bool),
                is_live[None, :] & (position[None, :] <= place_block[:, None]),
            ],
            axis=1,
        )
        scores = jnp.where(allowed[None], scores, -jnp.inf)
        row_max = jnp.max(scores, axis=-1, keepdims=True)
        weights = jnp.exp(scores - row_max)
        totals = jnp.sum(weights, axis=-1, keepdims=True)
        result = (
            jnp.einsum(
                "hrk,kd->hrd",
                weights.astype(jnp.bfloat16),
                value_all,
                preferred_element_type=jnp.float32,
            )
            / totals
        )
        return (
            result.astype(jnp.bfloat16).transpose(1, 0, 2).reshape(block_rows, per_dev * head_width)
        )

    attn_heads = lax.map(
        attend,
        (
            queries_by_head.reshape(block_count, block_rows, per_dev, head_width),
            position.reshape(block_count, block_rows),
        ),
    ).reshape(rows_of_group, per_dev * head_width)
    attn_sum = lax.psum_scatter(
        jnp.dot(attn_heads, out_weight, preferred_element_type=jnp.float32).astype(jnp.bfloat16),
        "sp",
        scatter_dimension=0,
        tiled=True,
    ).astype(jnp.float32)
    own_live = jnp.arange(slot_rows, dtype=jnp.int32) < lengths[0, 0]
    attended = jnp.where(own_live[:, None], attn_sum, 0.0).astype(jnp.bfloat16)
    mixed_rows = residual.astype(jnp.float32) + attn_sum
    normed = (
        mixed_rows
        * lax.rsqrt(jnp.mean(mixed_rows * mixed_rows, axis=-1, keepdims=True) + 1e-06)
        * norm_gain
    ).astype(jnp.bfloat16)
    group_count = lax.axis_size("grp")
    experts = up_gate_weight.shape[0] * group_count * seq_devices
    top_count = expert_ids.shape[1]
    capacity = max(2, 8 * slot_rows * top_count // (5 * experts))
    hidden_width = down_weight.shape[1]
    choose = expert_ids[:, :, None] == jnp.arange(experts, dtype=jnp.int32)[None, None, :]
    routed = (jnp.any(choose, axis=1) & own_live[:, None]).astype(jnp.float32)
    earlier = (jnp.arange(slot_rows)[:, None] > jnp.arange(slot_rows)[None, :]).astype(jnp.float32)
    prefix = jnp.dot(earlier, routed, precision=lax.Precision.HIGHEST)
    slot_in = jnp.sum(jnp.where(choose, prefix[:, None, :], 0.0), axis=2).astype(jnp.int32)
    dump_slot = experts * capacity
    target = jnp.where(own_live[:, None], expert_ids * capacity + slot_in, dump_slot)
    source_rows = (
        jnp.full((dump_slot + 1,), slot_rows, jnp.int32)
        .at[target.reshape(-1)]
        .set(jnp.repeat(jnp.arange(slot_rows, dtype=jnp.int32), top_count))[:dump_slot]
    )
    padded = jnp.concatenate([normed, jnp.zeros((1, model_width), jnp.bfloat16)], axis=0)
    outgoing = padded[source_rows].reshape(experts, capacity, model_width)
    received = lax.all_to_all(outgoing, ("grp", "sp"), split_axis=0, concat_axis=0, tiled=True)
    flat_rows = received.reshape(-1, model_width)
    projected = jnp.dot(flat_rows, up_gate_weight[0], preferred_element_type=jnp.float32)
    hidden = (jax.nn.silu(projected[:, :hidden_width]) * projected[:, hidden_width:]).astype(
        jnp.bfloat16
    )
    returned = lax.all_to_all(
        jnp.dot(hidden, down_weight[0], preferred_element_type=jnp.float32)
        .astype(jnp.bfloat16)
        .reshape(received.shape),
        ("grp", "sp"),
        split_axis=0,
        concat_axis=0,
        tiled=True,
    )
    back_rows = jnp.concatenate(
        [returned.reshape(dump_slot, model_width), jnp.zeros((1, model_width), jnp.bfloat16)],
        axis=0,
    )
    picked = back_rows[target]
    combined = jnp.sum(gate_values[:, :, None] * picked.astype(jnp.float32), axis=1)
    moe_out = jnp.where(own_live[:, None], combined, 0.0).astype(jnp.bfloat16)
    return (attended, moe_out)


def solution(mesh):
    in_specs = (
        P(("grp", "sp"), None),
        P(("grp", "sp"), None),
        P("grp", "sp", None, None),
        P("grp", "sp"),
        P("sp", None),
        P(("grp", "sp"), None),
        P(),
        P(("grp", "sp"), None),
        P(("grp", "sp"), None),
        P(("grp", "sp"), None, None),
        P(("grp", "sp"), None, None),
    )
    out_specs = (P(("grp", "sp"), None), P(("grp", "sp"), None))
    return jax.shard_map(
        per_device, mesh=mesh, in_specs=in_specs, out_specs=out_specs, check_vma=False
    )
```

profile of v0, /device:TPU:0, one launch (start us, length us, event | category | flops | bytes accessed | tf_op | source)
XLA Modules:
  0.0 589.6 jit_solution(7002747253154001575)
XLA Ops:
  8.0 1.2 fusion.44
  9.2 0.7 reshape.134
  9.9 0.9 copy.31
  10.8 0.7 reshape.135
  11.5 0.9 copy.32
  12.5 1.2 dynamic-slice.1
  13.7 0.8 maximum_bitcast_fusion
  14.5 0.7 bitcast_dynamic-update-slice_fusion
  15.1 4.2 all-to-all-start
  19.4 6.8 %all-reduce.3 = s32[4]{0:T(128)S(1)} all-reduce(s32[4]{0:T(128)S(1)} %bitcast_dynamic-update-slice_fusion), channel_id=1, replica_groups=mesh['grp'=8,'sp'=4] {'sp'}, use_global_device_ids=true, to_apply=%add.3 | all-reduce | flops 4 | bytes 32
  26.2 0.2 reduce-window_clone.1
  26.4 2.5 copy.50
  28.9 0.1 select_reduce_fusion.2
  29.0 4.3 all-to-all-start.1
  33.3 0.0 reduce-scatter.2.cloned.1.call-start
  33.4 0.3 compare_and_fusion
  33.8 1.0 concatenate.19
  34.8 1.7 fusion.45
  36.5 0.7 fusion.43
  37.2 13.5 %all-to-all-done.1 = bf16[160,4,1024]{2,0,1:T(8,128)(2,1)} async-done(((bf16[160,4,1024]{2,0,1:T(8,128)(2,1)}), bf16[160,4,1024]{2,0,1:T(8,128)(2,1)}, u32[]{:S(2)}, u32[]{:S(2)}) %all-to-all-start.1) | async-done | bytes 1310752 | tf_op jit(solution)/shard_map/all_to_all | solution.py:46
  50.7 1.7 copy.44
  52.4 11.2 %fusion.2 = (f32[8,640]{1,0:T(8,128)S(1)}, f32[1152,640,8]{1,0,2:T(8,128)}) fusion(pred[640,1152]{0,1:T(8,128)(4,1)} %concatenate.19, bf16[640,8,128]{2,1,0:T(8,128)(2,1)S(1)} %bitcast.67, bf16[640,128]{1,0:T(8,128)(2,1)} %get-tuple-element.33, bf16[512,128]{1,0:T(8,128)(2,1)} %get-tuple-element.37), kind=kOutput, calls=%fused_computation.7 | convolution fusion | flops 1528228864 | bytes 25956352 | tf_op jit(solution)/shard_map/while/body/eval_jaxpr/rhd,kd->hrk/dot_general | solution.py:77
  63.6 10.6 %fusion = f32[8,640]{1,0:T(8,128)S(1)} fusion(f32[1152,640,8]{1,0,2:T(8,128)} %get-tuple-element.39, f32[8,640]{1,0:T(8,128)S(1)} %get-tuple-element.38, pred[640,1152]{0,1:T(8,128)(4,1)S(1)} %copy-done.1), kind=kLoop, calls=%fused_computation.5 | loop fusion | flops 23587840 | bytes 24371200 | tf_op jit(solution)/shard_map/while/body/eval_jaxpr/reduce_sum | solution.py:90
  74.2 11.3 %fusion.13 = bf16[640,8,128]{0,2,1:T(8,128)(2,1)S(1)} fusion(f32[1152,640,8]{1,0,2:T(8,128)} %get-tuple-element.39, f32[8,640]{1,0:T(8,128)S(1)} %get-tuple-element.38, pred[640,1152]{0,1:T(8,128)(4,1)S(1)} %copy-done.1, f32[640,8]{0,1:T(8,128)S(1)} %bitcast.72, bf16[640,128]{1,0:T(8,128)(2,1)S(1)} %copy-done.2, bf16[512,128]{1,0:T(8,128)(2,1)S(1)} %copy-done.3), kind=kOutput, calls=%fused_computation.21 | convolution fusion | flops 1535442944 | bytes 25976832 | tf_op jit(solution)/shard_map/while/body/eval_jaxpr/hrk,kd->hrd/dot_general | solution.py:92
  85.6 4.2 convolution_convert_fusion.1
  89.9 0.1 fusion.24
  90.0 0.1 select_reduce_fusion
  90.1 0.1 copy.38
  90.2 0.1 reshape.137
  90.3 0.1 reshape.163
  90.5 5.4 scatter_custom_fusion
  95.9 29.6 %reduce-scatter.2.cloned.1.call-done = bf16[160,2048]{1,0:T(8,128)(2,1)} async-done(((bf16[640,2048]{1,0:T(8,128)(2,1)}), bf16[160,2048]{1,0:T(8,128)(2,1)}) %reduce-scatter.2.cloned.1.call-update) | async-done | bytes 655376 | tf_op jit(solution)/shard_map/reduce_scatter | solution.py:111
  125.6 1.6 multiply_reduce_fusion
  127.2 2.5 multiply_convert_fusion
  129.6 1.0 concatenate.23
  130.6 17.5 %gather_fusion = bf16[2048,2048]{1,0:T(8,128)(2,1)} fusion(bf16[161,2048]{1,0:T(8,128)(2,1)} %concatenate.23, s32[2048]{0:T(1024)S(1)} %fusion.27), kind=kCustom, calls=%fused_computation | custom fusion | bytes 16785408 | tf_op jit(solution)/shard_map/gather | solution.py:143
  148.1 188.2 %all_to_all.45 = bf16[32,64,2048]{2,1,0:T(8,128)(2,1)S(1)} all-to-all(bf16[32,64,2048]{2,1,0:T(8,128)(2,1)} %bitcast.64), channel_id=1, replica_groups=mesh['grp'=8,'sp'=4] {'grp','sp'}, dimensions={0} | all-to-all | bytes 16777216 | tf_op jit(solution)/shard_map/all_to_all | solution.py:144
  336.3 15.8 %fusion.8 = f32[2048,1536]{1,0:T(8,128)S(1)} fusion(bf16[2048,2048]{1,0:T(8,128)(2,1)S(1)} %bitcast.66, bf16[1,2048,1536]{2,1,0:T(8,128)(2,1)} %param.20), kind=kOutput, calls=%fused_computation.15 | convolution fusion | flops 12884901888 | bytes 27262976 | tf_op jit(solution)/shard_map/dot_general | solution.py:146
  352.1 8.9 %convolution_convert_fusion = bf16[2048,2048]{1,0:T(8,128)(2,1)} fusion(f32[2048,1536]{1,0:T(8,128)S(1)} %fusion.8, bf16[1,768,2048]{2,1,0:T(8,128)(2,1)S(1)} %copy-done), kind=kOutput, calls=%fused_computation.12 | convolution fusion | flops 6456082432 | bytes 24117248 | tf_op jit(solution)/shard_map/dot_general | solution.py:151
  361.0 4.2 all-to-all-start.3
  365.2 0.1 copy.39
  365.3 0.1 reshape.153
  365.4 0.1 copy.37
  365.6 184.7 %all-to-all-done.3 = bf16[32,64,2048]{2,1,0:T(8,128)(2,1)} async-done(((bf16[32,64,2048]{2,1,0:T(8,128)(2,1)}), bf16[32,64,2048]{2,1,0:T(8,128)(2,1)}, u32[]{:S(2)}, u32[]{:S(2)}) %all-to-all-start.3) | async-done | bytes 8388640 | tf_op jit(solution)/shard_map/all_to_all | solution.py:150
  550.3 8.3 %concatenate.24 = bf16[2049,2048]{1,0:T(8,128)(2,1)} pad(bf16[2048,2048]{1,0:T(8,128)(2,1)} %bitcast.22, bf16[]{:T(256)} %constant.67.clone.1), padding=0_1x0_0 | pad | bytes 16781314 | tf_op jit(solution)/shard_map/concatenate | solution.py:159
  558.5 15.3 %gather_fusion.1 = bf16[1280,2048]{1,0:T(8,128)(2,1)} fusion(bf16[2049,2048]{1,0:T(8,128)(2,1)} %concatenate.24, s32[2048]{0:T(1024)S(1)} %pad_clamp_fusion), kind=kCustom, calls=%fused_computation.1 | custom fusion | bytes 10490880 | tf_op jit(solution)/shard_map/gather | solution.py:163
  573.9 7.9 %fusion.6 = bf16[160,2048]{1,0:T(8,128)(2,1)S(1)} fusion(bf16[1280,2048]{1,0:T(8,128)(2,1)} %gather_fusion.1, f32[160,8]{1,0:T(8,128)S(1)} %copy.37), kind=kLoop, calls=%fused_computation.11 | loop fusion | flops 7536640 | bytes 5903360 | tf_op jit(solution)/shard_map/reduce_sum | solution.py:164
  581.8 1.0 select_convert_fusion
  (31 shorter events, 0.2 us)
Async XLA Ops:
  7.2 344.9 %copy-start = (bf16[1,768,2048]{2,1,0:T(8,128)(2,1)S(1)}, bf16[1,768,2048]{2,1,0:T(8,128)(2,1)}, u32[]{:S(2)}) copy-start(bf16[1,768,2048]{2,1,0:T(8,128)(2,1)} %param.21) | copy-start | bytes 9437188
  15.1 13.9 %all-to-all-start = ((bf16[160,4,256]{2,0,1:T(8,128)(2,1)}), bf16[160,4,256]{2,0,1:T(8,128)(2,1)S(1)}, u32[]{:S(2)}, u32[]{:S(2)}) async-start(bf16[160,4,256]{2,0,1:T(8,128)(2,1)} %maximum_bitcast_fusion), calls=%async_computation | async-start | bytes 655360 | tf_op jit(solution)/shard_map/all_to_all | solution.py:47
  29.0 21.6 %all-to-all-start.1 = ((bf16[160,4,1024]{2,0,1:T(8,128)(2,1)}), bf16[160,4,1024]{2,0,1:T(8,128)(2,1)}, u32[]{:S(2)}, u32[]{:S(2)}) async-start(bf16[160,4,1024]{2,0,1:T(8,128)(2,1)} %bitcast.68), calls=%async_computation.1 | async-start | bytes 2621440 | tf_op jit(solution)/shard_map/all_to_all | solution.py:46
  33.3 92.2 %reduce-scatter.2.cloned.1.call-start = ((), (), s32[]{:S(2)}) async-start(), calls=%async_computation.5 | async-start | bytes 3276800 | tf_op jit(solution)/shard_map/reduce_scatter | solution.py:111
  52.4 11.3 %copy-start.1 = (pred[640,1152]{0,1:T(8,128)(4,1)S(1)}, pred[640,1152]{0,1:T(8,128)(4,1)}, u32[]{:S(2)}) copy-start(pred[640,1152]{0,1:T(8,128)(4,1)} %concatenate.19) | copy-start | bytes 2211844
  63.6 10.6 %copy-start.2 = (bf16[640,128]{1,0:T(8,128)(2,1)S(1)}, bf16[640,128]{1,0:T(8,128)(2,1)}, u32[]{:S(2)}) copy-start(bf16[640,128]{1,0:T(8,128)(2,1)} %get-tuple-element.32) | copy-start | bytes 491524
  63.6 10.6 %copy-start.3 = (bf16[512,128]{1,0:T(8,128)(2,1)S(1)}, bf16[512,128]{1,0:T(8,128)(2,1)}, u32[]{:S(2)}) copy-start(bf16[512,128]{1,0:T(8,128)(2,1)} %get-tuple-element.36) | copy-start | bytes 393220
  74.2 11.3 %copy-start.7 = (bf16[1024,2048]{1,0:T(8,128)(2,1)S(1)}, bf16[1024,2048]{1,0:T(8,128)(2,1)}, u32[]{:S(2)}) copy-start(bf16[1024,2048]{1,0:T(8,128)(2,1)} %param.15) | copy-start | bytes 12582916
  85.6 4.3 copy-start.4
  85.6 41.6 %copy-start.5 = (f32[2048]{0:T(1024)S(1)}, f32[2048]{0:T(1024)}, u32[]{:S(2)}) copy-start(f32[2048]{0:T(1024)} %param.17) | copy-start | bytes 24580
  361.0 4.4 copy-start.6
  361.0 189.2 %all-to-all-start.3 = ((bf16[32,64,2048]{2,1,0:T(8,128)(2,1)}), bf16[32,64,2048]{2,1,0:T(8,128)(2,1)}, u32[]{:S(2)}, u32[]{:S(2)}) async-start(bf16[32,64,2048]{2,1,0:T(8,128)(2,1)} %bitcast.65), calls=%async_computation.4 | async-start | bytes 16777216 | tf_op jit(solution)/shard_map/all_to_all | solution.py:150
Sparse Core Ops, SparseCore 0:
  89.9 35.5 reduce-scatter.1
where the time goes:
time: 593 us; the launch traced here: 590 us
  waiting for transfers between devices  228 us (38%)
  blocking collectives  195 us (33%)
  local copies, waits for them, and re-layouts  62.2 us (10%)
  matrix products  51.6 us (9%)
  other arithmetic  25.1 us (4%)
  between operations  15.2 us (3%)
  starting transfers between devices  12.8 us (2%)
    all_to_all x1, blocking collectives, per_device(): lax.all_to_all(outgoing, ('grp', 'sp'), split_axis=0, concat_axis=0, tile...  188 us
    all_to_all x1, waiting for transfers between devices, per_device(): lax.all_to_all(jnp.dot(hidden, down_weight[0], preferred_element_type=jnp...  185 us
    reduce_scatter x1, waiting for transfers between devices, per_device(): lax.psum_scatter(jnp.dot(attn_heads, out_weight, preferred_element_type=j...  29.6 us
    gather x1, local copies, waits for them, and re-layouts, per_device(): outgoing = padded[source_rows].reshape(experts, capacity, model_width)  17.5 us
    dot_general x1, matrix products, per_device(): jnp.dot(flat_rows, up_gate_weight[0], preferred_element_type=jnp.float32)  15.8 us
    gather x1, local copies, waits for them, and re-layouts, per_device(): picked = back_rows[target]  15.3 us
    all_to_all x1, waiting for transfers between devices, per_device(): lax.all_to_all(queries, 'sp', split_axis=1, concat_axis=0, tiled=True)  13.5 us
  transfers between devices with their start and end apart: 4, of which 3 were waited for; matrix products, arithmetic and copies ran while one was open for 2% of the time, Pallas kernels for 0%

commit v1 on v0

--- a/solution.py
+++ b/solution.py
@@ -10,6 +10,97 @@
     mask = 2**bit
     pairs = [(source, source ^ mask) for source in range(lax.axis_size(axis))]
     return lax.ppermute(value, axis, pairs)
+
+
+def experts_by_exchange(
+    normed, own_live, expert_ids, gate_values, up_gate_weight, down_weight, capacity
+):
+    slot_rows, model_width = normed.shape
+    top_count = expert_ids.shape[1]
+    hidden_width = down_weight.shape[1]
+    experts = up_gate_weight.shape[0] * lax.axis_size(("grp", "sp"))
+    choose = expert_ids[:, :, None] == jnp.arange(experts, dtype=jnp.int32)[None, None, :]
+    routed = (jnp.any(choose, axis=1) & own_live[:, None]).astype(jnp.float32)
+    earlier = (jnp.arange(slot_rows)[:, None] > jnp.arange(slot_rows)[None, :]).astype(jnp.float32)
+    prefix = jnp.dot(earlier, routed, precision=lax.Precision.HIGHEST)
+    slot_in = jnp.sum(jnp.where(choose, prefix[:, None, :], 0.0), axis=2).astype(jnp.int32)
+    dump_slot = experts * capacity
+    target = jnp.where(own_live[:, None], expert_ids * capacity + slot_in, dump_slot)
+    source_rows = (
+        jnp.full((dump_slot + 1,), slot_rows, jnp.int32)
+        .at[target.reshape(-1)]
+        .set(jnp.repeat(jnp.arange(slot_rows, dtype=jnp.int32), top_count))[:dump_slot]
+    )
+    padded = jnp.concatenate([normed, jnp.zeros((1, model_width), jnp.bfloat16)], axis=0)
+    outgoing = padded[source_rows].reshape(experts, capacity, model_width)
+    received = lax.all_to_all(outgoing, ("grp", "sp"), split_axis=0, concat_axis=0, tiled=True)
+    flat_rows = received.reshape(-1, model_width)
+    projected = jnp.dot(flat_rows, up_gate_weight[0], preferred_element_type=jnp.float32)
+    hidden = (jax.nn.silu(projected[:, :hidden_width]) * projected[:, hidden_width:]).astype(
+        jnp.bfloat16
+    )
+    returned = lax.all_to_all(
+        jnp.dot(hidden, down_weight[0], preferred_element_type=jnp.float32)
+        .astype(jnp.bfloat16)
+        .reshape(received.shape),
+        ("grp", "sp"),
+        split_axis=0,
+        concat_axis=0,
+        tiled=True,
+    )
+    back_rows = jnp.concatenate(
+        [returned.reshape(dump_slot, model_width), jnp.zeros((1, model_width), jnp.bfloat16)],
+        axis=0,
+    )
+    picked = back_rows[target]
+    combined = jnp.sum(gate_values[:, :, None] * picked.astype(jnp.float32), axis=1)
+    moe_out = jnp.where(own_live[:, None], combined, 0.0).astype(jnp.bfloat16)
+    return moe_out
+
+
+def experts_by_gather(
+    normed, own_live, expert_ids, gate_values, up_gate_weight, down_weight, capacity
+):
+    axes = ("grp", "sp")
+    slot_rows, model_width = normed.shape
+    hidden_width = down_weight.shape[1]
+    devices = lax.axis_size(axes)
+    mine = lax.axis_index(axes)
+    live_ids = jnp.where(own_live[:, None], expert_ids, -1)
+    ids_all = lax.all_gather(live_ids, axes, axis=0, tiled=False)
+    gates_all = lax.all_gather(gate_values, axes, axis=0, tiled=False)
+    chosen = ids_all == mine
+    wanted = jnp.any(chosen, axis=2)
+    gate = jnp.sum(jnp.where(chosen, gates_all, 0.0), axis=2)
+    place = jnp.cumsum(wanted.astype(jnp.int32), axis=1) - 1
+    pick = wanted[:, None, :] & (
+        place[:, None, :] == jnp.arange(capacity, dtype=jnp.int32)[None, :, None]
+    )
+    rows_all = lax.all_gather(normed, axes, axis=0, tiled=False)
+    picked = jnp.einsum(
+        "bsr,brd->bsd", pick.astype(jnp.bfloat16), rows_all, preferred_element_type=jnp.float32
+    ).astype(jnp.bfloat16)
+    projected = jnp.dot(
+        picked.reshape(devices * capacity, model_width),
+        up_gate_weight[0],
+        preferred_element_type=jnp.float32,
+    )
+    hidden = (jax.nn.silu(projected[:, :hidden_width]) * projected[:, hidden_width:]).astype(
+        jnp.bfloat16
+    )
+    result = jnp.dot(hidden, down_weight[0], preferred_element_type=jnp.float32).astype(
+        jnp.bfloat16
+    )
+    weight = jnp.where(pick, gate[:, None, :], 0.0).astype(jnp.bfloat16)
+    share = jnp.einsum(
+        "bsr,bsd->brd",
+        weight,
+        result.reshape(devices, capacity, model_width),
+        preferred_element_type=jnp.float32,
+    ).astype(jnp.bfloat16)
+    return lax.psum_scatter(
+        share.reshape(devices * slot_rows, model_width), axes, scatter_dimension=0, tiled=True
+    )
 
 
 def per_device(
@@ -126,43 +217,14 @@
     experts = up_gate_weight.shape[0] * group_count * seq_devices
     top_count = expert_ids.shape[1]
     capacity = max(2, 8 * slot_rows * top_count // (5 * experts))
-    hidden_width = down_weight.shape[1]
-    choose = expert_ids[:, :, None] == jnp.arange(experts, dtype=jnp.int32)[None, None, :]
-    routed = (jnp.any(choose, axis=1) & own_live[:, None]).astype(jnp.float32)
-    earlier = (jnp.arange(slot_rows)[:, None] > jnp.arange(slot_rows)[None, :]).astype(jnp.float32)
-    prefix = jnp.dot(earlier, routed, precision=lax.Precision.HIGHEST)
-    slot_in = jnp.sum(jnp.where(choose, prefix[:, None, :], 0.0), axis=2).astype(jnp.int32)
-    dump_slot = experts * capacity
-    target = jnp.where(own_live[:, None], expert_ids * capacity + slot_in, dump_slot)
-    source_rows = (
-        jnp.full((dump_slot + 1,), slot_rows, jnp.int32)
-        .at[target.reshape(-1)]
-        .set(jnp.repeat(jnp.arange(slot_rows, dtype=jnp.int32), top_count))[:dump_slot]
-    )
-    padded = jnp.concatenate([normed, jnp.zeros((1, model_width), jnp.bfloat16)], axis=0)
-    outgoing = padded[source_rows].reshape(experts, capacity, model_width)
-    received = lax.all_to_all(outgoing, ("grp", "sp"), split_axis=0, concat_axis=0, tiled=True)
-    flat_rows = received.reshape(-1, model_width)
-    projected = jnp.dot(flat_rows, up_gate_weight[0], preferred_element_type=jnp.float32)
-    hidden = (jax.nn.silu(projected[:, :hidden_width]) * projected[:, hidden_width:]).astype(
-        jnp.bfloat16
-    )
-    returned = lax.all_to_all(
-        jnp.dot(hidden, down_weight[0], preferred_element_type=jnp.float32)
-        .astype(jnp.bfloat16)
-        .reshape(received.shape),
-        ("grp", "sp"),
-        split_axis=0,
-        concat_axis=0,
-        tiled=True,
-    )
-    back_rows = jnp.concatenate(
-        [returned.reshape(dump_slot, model_width), jnp.zeros((1, model_width), jnp.bfloat16)],
-        axis=0,
-    )
-    picked = back_rows[target]
-    combined = jnp.sum(gate_values[:, :, None] * picked.astype(jnp.float32), axis=1)
-    moe_out = jnp.where(own_live[:, None], combined, 0.0).astype(jnp.bfloat16)
+    if experts <= 4 * top_count:
+        moe_out = experts_by_gather(
+            normed, own_live, expert_ids, gate_values, up_gate_weight, down_weight, capacity
+        )
+    else:
+        moe_out = experts_by_exchange(
+            normed, own_live, expert_ids, gate_values, up_gate_weight, down_weight, capacity
+        )
     return (attended, moe_out)
 
 

time: 593 us -> 551 us (0.929)
  blocking collectives: 195 us -> 87.1 us
  waiting for transfers between devices: 228 us -> 328 us
  local copies, waits for them, and re-layouts: 62.2 us -> 14.2 us
  matrix products: 51.6 us -> 78.2 us
  other arithmetic: 25.1 us -> 17.4 us
    reduce_scatter x0 -> x1, waiting for transfers between devices: none -> 224 us  [experts_by_gather(): lax.psum_scatter(share.reshape(devices * slot_rows, model_width), axes, s...]
    all_to_all x1 -> x0, blocking collectives: 188 us -> none  [per_device(): lax.all_to_all(outgoing, ('grp', 'sp'), split_axis=0, concat_axis=0, tile...]
    all_to_all x1 -> x0, waiting for transfers between devices: 185 us -> none  [per_device(): lax.all_to_all(jnp.dot(hidden, down_weight[0], preferred_element_type=jnp...]
    all_gather x0 -> x2, blocking collectives: none -> 80.3 us  [the longest x1 42.2 us: experts_by_gather(): ids_all = lax.all_gather(live_ids, axes, axis=0, tiled=False)]
    all_gather x0 -> x1, waiting for transfers between devices: none -> 55 us  [experts_by_gather(): rows_all = lax.all_gather(normed, axes, axis=0, tiled=False)]
    gather x2 -> x0, local copies, waits for them, and re-layouts: 32.9 us -> none  [the longest x1 17.5 us: per_device(): outgoing = padded[source_rows].reshape(experts, capacity, model_width)]
    dot_general x3 -> x4, matrix products: 24.8 us -> 51.5 us  [the longest x1 17.4 us: experts_by_gather(): jnp.dot(picked.reshape(devices * capacity, model_width), up_gate_weight[0...]
    concatenate x2 -> x0, local copies, waits for them, and re-layouts: 9.26 us -> none  [the longest x1 8.27 us: per_device(): jnp.concatenate([returned.reshape(dump_slot, model_width), jnp.zeros((1,...]
  transfers between devices with their start and end apart: 4 -> 5, of which waited for: 3 -> 4; matrix products, arithmetic and copies ran while one was open for 2% -> 1% of each run, Pallas kernels for 0% -> 0%
where the time goes in v1:
time: 551 us; the launch traced here: 548 us
  waiting for transfers between devices  328 us (60%)
  blocking collectives  87.1 us (16%)
  matrix products  78.2 us (14%)
  other arithmetic  17.4 us (3%)
  between operations  14.8 us (3%)
  local copies, waits for them, and re-layouts  14.2 us (3%)
  starting transfers between devices  8.66 us (2%)
    reduce_scatter x1, waiting for transfers between devices, experts_by_gather(): lax.psum_scatter(share.reshape(devices * slot_rows, model_width), axes, s...  224 us
    all_gather x1, waiting for transfers between devices, experts_by_gather(): rows_all = lax.all_gather(normed, axes, axis=0, tiled=False)  55 us
    all_gather x1, blocking collectives, experts_by_gather(): ids_all = lax.all_gather(live_ids, axes, axis=0, tiled=False)  42.2 us
    all_gather x1, blocking collectives, experts_by_gather(): gates_all = lax.all_gather(gate_values, axes, axis=0, tiled=False)  38.1 us
    reduce_scatter x1, waiting for transfers between devices, per_device(): lax.psum_scatter(jnp.dot(attn_heads, out_weight, preferred_element_type=j...  35.7 us
    dot_general x1, matrix products, experts_by_gather(): jnp.dot(picked.reshape(devices * capacity, model_width), up_gate_weight[0...  17.4 us
    all_to_all x1, waiting for transfers between devices, per_device(): lax.all_to_all(queries, 'sp', split_axis=1, concat_axis=0, tiled=True)  13.5 us
    dot_general x1, matrix products, experts_by_gather(): jnp.einsum('bsr,brd->bsd', pick.astype(jnp.bfloat16), rows_all, preferred...  13.1 us
  transfers between devices with their start and end apart: 5, of which 4 were waited for; matrix products, arithmetic and copies ran while one was open for 1% of the time, Pallas kernels for 0%

profile of v1, /device:TPU:0, one launch (start us, length us, event | category | flops | bytes accessed | tf_op | source)
XLA Modules:
  0.0 548.2 jit_solution(12908728536935020054)
XLA Ops:
  7.2 0.0 copy-start
  8.0 1.2 fusion.44
  9.2 0.7 reshape.108
  9.9 0.9 copy.33
  10.8 0.7 reshape.109
  11.5 0.9 copy.34
  12.5 1.2 dynamic-slice.1
  13.7 0.8 maximum_bitcast_fusion
  14.5 0.7 bitcast_dynamic-update-slice_fusion
  15.1 4.2 all-to-all-start
  19.4 6.8 %all-reduce.2 = s32[4]{0:T(128)S(1)} all-reduce(s32[4]{0:T(128)S(1)} %bitcast_dynamic-update-slice_fusion), channel_id=1, replica_groups=mesh['grp'=8,'sp'=4] {'sp'}, use_global_device_ids=true, to_apply=%add.2 | all-reduce | flops 4 | bytes 32
  26.2 0.2 reduce-window_clone.1
  26.4 2.5 copy.55
  28.9 0.1 select_reduce_fusion.2
  29.0 4.3 all-to-all-start.1
  33.3 0.0 reduce-scatter.3.cloned.1.call-start
  33.4 0.3 compare_and_fusion
  33.8 1.0 concatenate.13
  34.8 1.7 fusion.45
  36.5 0.7 fusion.43
  37.2 13.5 %all-to-all-done.1 = bf16[160,4,1024]{2,0,1:T(8,128)(2,1)} async-done(((bf16[160,4,1024]{2,0,1:T(8,128)(2,1)}), bf16[160,4,1024]{2,0,1:T(8,128)(2,1)}, u32[]{:S(2)}, u32[]{:S(2)}) %all-to-all-start.1) | async-done | bytes 1310752 | tf_op jit(solution)/shard_map/all_to_all | solution.py:137
  50.7 1.7 copy.47
  52.4 11.2 %fusion.2 = (f32[8,640]{1,0:T(8,128)S(1)}, f32[1152,640,8]{1,0,2:T(8,128)}) fusion(pred[640,1152]{0,1:T(8,128)(4,1)} %concatenate.13, bf16[640,8,128]{2,1,0:T(8,128)(2,1)S(1)} %bitcast.80, bf16[640,128]{1,0:T(8,128)(2,1)} %get-tuple-element.33, bf16[512,128]{1,0:T(8,128)(2,1)} %get-tuple-element.37), kind=kOutput, calls=%fused_computation.4 | convolution fusion | flops 1528228864 | bytes 25956352 | tf_op jit(solution)/shard_map/while/body/eval_jaxpr/rhd,kd->hrk/dot_general | solution.py:168
  63.6 10.6 %fusion = f32[8,640]{1,0:T(8,128)S(1)} fusion(f32[1152,640,8]{1,0,2:T(8,128)} %get-tuple-element.39, f32[8,640]{1,0:T(8,128)S(1)} %get-tuple-element.38, pred[640,1152]{0,1:T(8,128)(4,1)S(1)} %copy-done.1), kind=kLoop, calls=%fused_computation.2 | loop fusion | flops 23587840 | bytes 24371200 | tf_op jit(solution)/shard_map/while/body/eval_jaxpr/reduce_sum | solution.py:181
  74.2 0.0 copy-start.7
  74.2 11.3 %fusion.12 = bf16[640,8,128]{0,2,1:T(8,128)(2,1)S(1)} fusion(f32[1152,640,8]{1,0,2:T(8,128)} %get-tuple-element.39, f32[8,640]{1,0:T(8,128)S(1)} %get-tuple-element.38, pred[640,1152]{0,1:T(8,128)(4,1)S(1)} %copy-done.1, f32[640,8]{0,1:T(8,128)S(1)} %bitcast.85, bf16[640,128]{1,0:T(8,128)(2,1)S(1)} %copy-done.2, bf16[512,128]{1,0:T(8,128)(2,1)S(1)} %copy-done.3), kind=kOutput, calls=%fused_computation.18 | convolution fusion | flops 1535442944 | bytes 25976832 | tf_op jit(solution)/shard_map/while/body/eval_jaxpr/hrk,kd->hrd/dot_general | solution.py:183
  85.6 4.2 convolution_convert_fusion.3
  89.8 0.0 reduce-scatter.3.cloned.1.call-update
  89.8 0.0 all-gather.7.cloned.1.call-start
  89.8 35.7 %reduce-scatter.3.cloned.1.call-done = bf16[160,2048]{1,0:T(8,128)(2,1)} async-done(((bf16[640,2048]{1,0:T(8,128)(2,1)}), bf16[160,2048]{1,0:T(8,128)(2,1)}) %reduce-scatter.3.cloned.1.call-update) | async-done | bytes 655376 | tf_op jit(solution)/shard_map/reduce_scatter | solution.py:202
  125.5 1.6 multiply_reduce_fusion
  127.1 2.7 multiply_convert_fusion
  129.8 0.0 all-gather.7.cloned.1.call-update
  129.9 0.0 reduce-scatter.5.cloned.1.call-start
  129.9 42.2 %all-gather.3 = s32[32,160,8]{1,2,0:T(8,128)S(1)} all-gather(s32[1,160,8]{1,2,0:T(8,128)S(1)} %select_bitcast_fusion), channel_id=2, replica_groups=mesh['grp'=8,'sp'=4] {'grp','sp'}, dimensions={0}, use_global_device_ids=true | all-gather | bytes 168960 | tf_op jit(solution)/shard_map/all_gather | solution.py:70
  172.1 38.1 %all-gather.4 = f32[32,160,8]{1,2,0:T(8,128)S(1)} all-gather(f32[1,160,8]{1,2,0:T(8,128)S(1)} %bitcast.86), channel_id=3, replica_groups=mesh['grp'=8,'sp'=4] {'grp','sp'}, dimensions={0}, use_global_device_ids=true | all-gather | bytes 168960 | tf_op jit(solution)/shard_map/all_gather | solution.py:71
  210.2 0.1 select_reduce_fusion
  210.3 0.1 reduce.2
  210.4 0.8 reduce-window.9
  211.2 0.2 slice_reduce_fusion
  211.4 0.1 copy_bitcast_fusion.1
  211.5 55.0 %all-gather.7.cloned.1.call-done = bf16[5120,2048]{1,0:T(8,128)(2,1)} async-done(((bf16[160,2048]{1,0:T(8,128)(2,1)}), bf16[5120,2048]{1,0:T(8,128)(2,1)}) %all-gather.7.cloned.1.call-update) | async-done | bytes 20971536 | tf_op jit(solution)/shard_map/all_gather | solution.py:79
  266.6 13.1 %convolution_convert_fusion.2 = bf16[32,64,2048]{2,1,0:T(8,128)(2,1)} fusion(bf16[32,160,2048]{2,1,0:T(8,128)(2,1)} %bitcast.77, s32[32,160]{1,0:T(8,128)S(1)} %slice_add_fusion, pred[32,160]{1,0:T(8,128)(4,1)S(1)} %reduce.2), kind=kOutput, calls=%fused_computation.13 | convolution fusion | flops 1347026944 | bytes 29385728 | tf_op jit(solution)/shard_map/bsr,brd->bsd/dot_general | solution.py:80
  279.7 17.4 %fusion.7 = f32[2048,1536]{1,0:T(8,128)S(1)} fusion(bf16[2048,2048]{1,0:T(8,128)(2,1)} %bitcast.79, bf16[1,2048,1536]{2,1,0:T(8,128)(2,1)} %param.20), kind=kOutput, calls=%fused_computation.11 | convolution fusion | flops 12884901888 | bytes 27262976 | tf_op jit(solution)/shard_map/dot_general | solution.py:83
  297.1 8.9 %convolution_convert_fusion.1 = bf16[2048,2048]{1,0:T(8,128)(2,1)} fusion(f32[2048,1536]{1,0:T(8,128)S(1)} %fusion.7, bf16[1,768,2048]{2,1,0:T(8,128)(2,1)S(1)} %copy-done), kind=kOutput, calls=%fused_computation.8 | convolution fusion | flops 6456082432 | bytes 24117248 | tf_op jit(solution)/shard_map/dot_general | solution.py:91
  306.0 12.1 %convolution_convert_fusion = bf16[32,160,2048]{2,1,0:T(8,128)(2,1)} fusion(bf16[32,64,2048]{2,1,0:T(8,128)(2,1)} %bitcast.78, bf16[32,160]{1,0:T(8,128)(2,1)S(1)} %get-tuple-element.20, s32[32,160]{1,0:T(8,128)S(1)} %slice_add_fusion, pred[32,160]{1,0:T(8,128)(4,1)S(1)} %reduce.2), kind=kOutput, calls=%fused_computation.5 | convolution fusion | flops 1353646080 | bytes 29395968 | tf_op jit(solution)/shard_map/bsr,bsd->brd/dot_general | solution.py:95
  318.1 0.0 reduce-scatter.5.cloned.1.call-update
  318.1 223.6 %reduce-scatter.5.cloned.1.call-done = bf16[160,2048]{1,0:T(8,128)(2,1)} async-done(((bf16[5120,2048]{1,0:T(8,128)(2,1)}), bf16[160,2048]{1,0:T(8,128)(2,1)}) %reduce-scatter.5.cloned.1.call-update) | async-done | bytes 655376 | tf_op jit(solution)/shard_map/reduce_scatter | solution.py:101
  (27 shorter events, 0.2 us)
Async XLA Ops:
  7.2 289.9 %copy-start = (bf16[1,768,2048]{2,1,0:T(8,128)(2,1)S(1)}, bf16[1,768,2048]{2,1,0:T(8,128)(2,1)}, u32[]{:S(2)}) copy-start(bf16[1,768,2048]{2,1,0:T(8,128)(2,1)} %param.21) | copy-start | bytes 9437188
  15.1 13.9 %all-to-all-start = ((bf16[160,4,256]{2,0,1:T(8,128)(2,1)}), bf16[160,4,256]{2,0,1:T(8,128)(2,1)S(1)}, u32[]{:S(2)}, u32[]{:S(2)}) async-start(bf16[160,4,256]{2,0,1:T(8,128)(2,1)} %maximum_bitcast_fusion), calls=%async_computation | async-start | bytes 655360 | tf_op jit(solution)/shard_map/all_to_all | solution.py:138
  29.0 21.6 %all-to-all-start.1 = ((bf16[160,4,1024]{2,0,1:T(8,128)(2,1)}), bf16[160,4,1024]{2,0,1:T(8,128)(2,1)}, u32[]{:S(2)}, u32[]{:S(2)}) async-start(bf16[160,4,1024]{2,0,1:T(8,128)(2,1)} %bitcast.81), calls=%async_computation.1 | async-start | bytes 2621440 | tf_op jit(solution)/shard_map/all_to_all | solution.py:137
  33.3 92.2 %reduce-scatter.3.cloned.1.call-start = ((), (), s32[]{:S(2)}) async-start(), calls=%async_computation.4 | async-start | bytes 3276800 | tf_op jit(solution)/shard_map/reduce_scatter | solution.py:202
  52.4 11.3 %copy-start.1 = (pred[640,1152]{0,1:T(8,128)(4,1)S(1)}, pred[640,1152]{0,1:T(8,128)(4,1)}, u32[]{:S(2)}) copy-start(pred[640,1152]{0,1:T(8,128)(4,1)} %concatenate.13) | copy-start | bytes 2211844
  63.6 10.6 %copy-start.2 = (bf16[640,128]{1,0:T(8,128)(2,1)S(1)}, bf16[640,128]{1,0:T(8,128)(2,1)}, u32[]{:S(2)}) copy-start(bf16[640,128]{1,0:T(8,128)(2,1)} %get-tuple-element.32) | copy-start | bytes 491524
  63.6 10.6 %copy-start.3 = (bf16[512,128]{1,0:T(8,128)(2,1)S(1)}, bf16[512,128]{1,0:T(8,128)(2,1)}, u32[]{:S(2)}) copy-start(bf16[512,128]{1,0:T(8,128)(2,1)} %get-tuple-element.36) | copy-start | bytes 393220
  74.2 11.3 %copy-start.7 = (bf16[1024,2048]{1,0:T(8,128)(2,1)S(1)}, bf16[1024,2048]{1,0:T(8,128)(2,1)}, u32[]{:S(2)}) copy-start(bf16[1024,2048]{1,0:T(8,128)(2,1)} %param.15) | copy-start | bytes 12582916
  85.6 41.6 %copy-start.4 = (f32[2048]{0:T(1024)S(1)}, f32[2048]{0:T(1024)}, u32[]{:S(2)}) copy-start(f32[2048]{0:T(1024)} %param.17) | copy-start | bytes 24580
  89.8 40.2 %copy-start.6 = (s32[160,8]{0,1:T(8,128)S(1)}, s32[160,8]{0,1:T(8,128)}, u32[]{:S(2)}) copy-start(s32[160,8]{0,1:T(8,128)} %param.18) | copy-start | bytes 15364
  89.8 82.4 %copy-start.5 = (f32[160,8]{0,1:T(8,128)S(1)}, f32[160,8]{0,1:T(8,128)}, u32[]{:S(2)}) copy-start(f32[160,8]{0,1:T(8,128)} %param.19) | copy-start | bytes 15364
  89.8 176.8 %all-gather.7.cloned.1.call-start = ((), (), s32[]{:S(2)}) async-start(), calls=%async_computation.6 | async-start | bytes 21626880 | tf_op jit(solution)/shard_map/all_gather | solution.py:79
  129.9 411.8 %reduce-scatter.5.cloned.1.call-start = ((), (), s32[]{:S(2)}) async-start(), calls=%async_computation.5 | async-start | bytes 21626880 | tf_op jit(solution)/shard_map/reduce_scatter | solution.py:101
Sparse Core Ops, SparseCore 0:
  89.9 35.5 reduce-scatter.2
  130.0 136.5 all-gather.6
  318.2 223.4 reduce-scatter.4
